TPU v7x, 32 devices: a whole 2x2x4 slice. The times are simulated.
32 devices in a mesh: bev: 8 (over z, x), scene: 4 (over y, core).
Axes of the slice: x: 2, y: 2, z: 4, core: 2. Of those that a mesh axis runs over, the one named last changes fastest.
Arguments:
- context: bfloat16 [4, 80, 2048], P('scene', None, 'bev'), may hold values from -24 to 24
- depth_logits: float32 [4, 112, 2048], P('scene', None, 'bev'), may hold values from -20 to 300
- send_count: int32 [4, 8, 8], P('scene', 'bev'), may hold values from 0 to 1024, as said below
- slot_point: int32 [4, 8, 8, 1024], P('scene', 'bev'), may hold values from 0 to 28671, as said below
- slot_cell: int32 [4, 8, 8, 1024], P('scene', 'bev'), may hold values from 0 to 2047
Outputs:
- bev_features: bfloat16 [16384, 320], P(('bev', 'scene'))
Inputs may be any that keep to these rules, and one draw needn't show every extreme that they name: `send_count`: one entry is 1024 in every pixel block's row. `slot_point`: the live slots of one pixel block name distinct points; slots at or past the count are unused.
All inputs are finite; a program needn't handle non-finite values.
Results may differ from a plain program's by a relative error of at most 0.0062.
Values may be sent and summed in bfloat16 or wider, within the bound.
A program may use at most 128 MiB of HBM per device.

v0:
```python
import jax
import jax.numpy as jnp
from jax import lax
from jax.sharding import PartitionSpec as P

GRID = 128


def pool_total(values, cell_ids, strip_cells):
    onehot = (
        cell_ids[:, :, None] == jnp.arange(strip_cells, dtype=jnp.int32)[None, None, :]
    ).astype(jnp.bfloat16)
    return jnp.einsum("gcs,gsn->nc", values, onehot, preferred_element_type=jnp.float32)


def select_points(point_ids, context_map, depth_prob):
    pix_block = context_map.shape[1]
    depth_bins = depth_prob.shape[0]
    depth_bin = point_ids // pix_block
    pixel_ids = point_ids % pix_block
    pixel_hot = (
        pixel_ids[:, :, None] == jnp.arange(pix_block, dtype=jnp.int32)[None, None, :]
    ).astype(jnp.bfloat16)
    depth_hot = (
        depth_bin[:, :, None] == jnp.arange(depth_bins, dtype=jnp.int32)[None, None, :]
    ).astype(jnp.bfloat16)
    features = jnp.einsum("nsp,cp->ncs", pixel_hot, context_map, preferred_element_type=jnp.float32)
    prob_rows = jnp.einsum("nsk,kp->nsp", depth_hot, depth_prob, preferred_element_type=jnp.float32)
    weight = jnp.sum(prob_rows * pixel_hot.astype(jnp.float32), axis=2)
    return (features * weight[:, None, :]).astype(jnp.bfloat16)


def body(context, depth_logits, send_count, slot_point, slot_cell):
    strips = lax.axis_size("bev")
    scenes = lax.axis_size("scene")
    strip_cells = GRID * GRID // strips
    channels = context.shape[1]
    capacity = slot_point.shape[3]
    depth_prob = jax.nn.softmax(depth_logits[0], axis=0).astype(jnp.bfloat16)
    context_map = context[0]
    counts = send_count[0, 0]
    points = slot_point[0, 0]
    live_mask = jnp.arange(capacity, dtype=jnp.int32)[None, :] < counts[:, None]
    targets = jnp.where(live_mask, slot_cell[0, 0], strip_cells)
    group_size = 8
    grouped = points.reshape(strips // group_size, group_size, capacity)
    values = lax.map(lambda ids: select_points(ids, context_map, depth_prob), grouped)
    values = values.reshape(strips, channels, capacity)
    got_values, got_cells = (
        lax.all_to_all(values, "bev", split_axis=0, concat_axis=0, tiled=True),
        lax.all_to_all(targets, "bev", split_axis=0, concat_axis=0, tiled=True),
    )
    got_values = got_values.reshape(strips // group_size, group_size, channels, capacity)
    got_cells = got_cells.reshape(strips // group_size, group_size, capacity)

    def add_group(running, blocks):
        return (running + pool_total(blocks[0], blocks[1], strip_cells), None)

    strip_sum, _ = lax.scan(
        add_group, jnp.zeros((strip_cells, channels), jnp.float32), (got_values, got_cells)
    )
    quarter = strip_cells // scenes
    rounded = strip_sum.astype(jnp.bfloat16).reshape(scenes, quarter, 1, channels)
    moved = lax.all_to_all(rounded, "scene", split_axis=0, concat_axis=2, tiled=True)
    return moved.reshape(quarter, scenes * channels)


def solution(mesh):
    return jax.shard_map(
        body,
        mesh=mesh,
        in_specs=(
            P("scene", None, "bev"),
            P("scene", None, "bev"),
            P("scene", "bev", None),
            P("scene", "bev", None, None),
            P("scene", "bev", None, None),
        ),
        out_specs=P(("bev", "scene"), None),
        check_vma=False,
    )
```

profile of v0, /device:TPU:1, one launch (start us, length us, event | category | flops | bytes accessed | tf_op | source)
XLA Modules:
  0.0 80.0 jit_solution(6481556922405416130)
XLA Ops:
  0.0 0.0 copy-start
  0.0 1.5 %compare_select_fusion = s32[8,1,1024]{2,1,0:T(1,128)} fusion(s32[1,1,8,1024]{3,2,1,0:T(8,128)} %param.9, s32[8]{0:T(128)} %bitcast.65), kind=kLoop, calls=%fused_computation.15 | loop fusion | flops 16384 | bytes 65568 | tf_op jit(solution)/shard_map/jit(_where)/select_n | solution.py:44
  1.5 6.4 %all-to-all-start = ((s32[8,1,1024]{2,1,0:T(1,128)}), s32[8,1,1024]{2,1,0:T(1,128)S(1)}, u32[]{:S(2)}, u32[]{:S(2)}) async-start(s32[8,1,1024]{2,1,0:T(1,128)} %compare_select_fusion), calls=%async_computation | async-start | bytes 65536 | tf_op jit(solution)/shard_map/all_to_all | solution.py:51
  7.8 0.8 add_select_fusion
  8.6 0.9 %reduce_max.9 = f32[256]{0:T(256)S(1)} reduce(f32[1,112,256]{2,1,0:T(8,128)} %param.6, f32[]{:T(128)} %constant.54.clone.1), dimensions={0,1}, to_apply=%region_0.0 | reduce | flops 28416 | bytes 115716 | tf_op jit(solution)/shard_map/reduce_max | solution.py:39
  9.6 0.9 %fusion.11 = f32[256]{0:T(256)S(1)} fusion(f32[1,112,256]{2,1,0:T(8,128)} %param.6, f32[256]{0:T(256)S(1)} %reduce_max.9), kind=kLoop, calls=%fused_computation.19 | loop fusion | flops 57088 | bytes 116736 | tf_op jit(solution)/shard_map/reduce_sum | solution.py:39
  10.5 3.2 %multiply_reduce_fusion = f32[8,1024]{1,0:T(8,128)S(1)} fusion(s32[8,1024]{1,0:T(8,128)S(1)} %get-tuple-element.23, s32[8,1024]{1,0:T(8,128)S(1)} %get-tuple-element.22, f32[1,112,256]{2,1,0:T(8,128)} %param.6, f32[256]{0:T(256)S(1)} %fusion.11, f32[256]{0:T(256)S(1)} %reduce_max.9), kind=kOutput, calls=%fused_computation.3 | convolution fusion | flops 481243136 | bytes 215040 | tf_op jit(solution)/shard_map/while/body/eval_jaxpr/nsk,kp->nsp/dot_general | solution.py:28
  13.7 0.0 copy-done
  13.8 2.9 %fusion.9 = bf16[8,80,1024]{2,1,0:T(8,128)(2,1)} fusion(s32[8,1024]{1,0:T(8,128)S(1)} %get-tuple-element.23, f32[8,1024]{1,0:T(8,128)S(1)} %multiply_reduce_fusion, bf16[1,80,256]{2,1,0:T(8,128)(2,1)S(1)} %copy-done), kind=kOutput, calls=%fused_computation.14 | convolution fusion | flops 338952192 | bytes 1417216 | tf_op jit(solution)/shard_map/while/body/eval_jaxpr/nsp,cp->ncs/dot_general | solution.py:27
  16.7 0.0 all-to-all-done
  16.7 5.4 %all-to-all-start.1 = ((bf16[8,80,1024]{2,1,0:T(8,128)(2,1)}), bf16[8,80,1024]{2,1,0:T(8,128)(2,1)S(1)}, u32[]{:S(2)}, u32[]{:S(2)}) async-start(bf16[8,80,1024]{2,1,0:T(8,128)(2,1)} %fusion.9), calls=%async_computation.1 | async-start | bytes 2621440 | tf_op jit(solution)/shard_map/all_to_all | solution.py:50
  22.1 29.9 %all-to-all-done.1 = bf16[8,80,1024]{2,1,0:T(8,128)(2,1)S(1)} async-done(((bf16[8,80,1024]{2,1,0:T(8,128)(2,1)}), bf16[8,80,1024]{2,1,0:T(8,128)(2,1)S(1)}, u32[]{:S(2)}, u32[]{:S(2)}) %all-to-all-start.1) | async-done | bytes 1310752 | tf_op jit(solution)/shard_map/all_to_all | solution.py:50
  52.0 15.9 %fusion.7 = bf16[2048,80]{0,1:T(8,128)(2,1)S(1)} fusion(bf16[8,80,1024]{2,1,0:T(8,128)(2,1)S(1)} %all-to-all-done.1, s32[8,1024]{1,0:T(8,128)S(1)} %bitcast.64), kind=kOutput, calls=%fused_computation.12 | convolution fusion | flops 2701295616 | bytes 1671168 | tf_op jit(solution)/shard_map/while/body/eval_jaxpr/gcs,gsn->nc/dot_general | solution.py:13
  67.8 0.2 reshape.121
  68.1 0.1 copy.10
  68.1 11.2 %all_to_all.26 = bf16[4,512,1,80]{1,3,2,0:T(8,128)(2,1)S(1)} all-to-all(bf16[4,512,1,80]{1,3,2,0:T(8,128)(2,1)S(1)} %copy.10), channel_id=1, replica_groups=mesh['bev'=8,'scene'=4] {'scene'}, dimensions={0} | all-to-all | bytes 655360 | tf_op jit(solution)/shard_map/all_to_all | solution.py:64
  79.3 0.7 copy.17
  (1 shorter events, 0.0 us)
Async XLA Ops:
  0.0 13.7 %copy-start = (bf16[1,80,256]{2,1,0:T(8,128)(2,1)S(1)}, bf16[1,80,256]{2,1,0:T(8,128)(2,1)}, u32[]{:S(2)}) copy-start(bf16[1,80,256]{2,1,0:T(8,128)(2,1)} %param.5) | copy-start | bytes 122884
  1.5 15.2 %all-to-all-start = ((s32[8,1,1024]{2,1,0:T(1,128)}), s32[8,1,1024]{2,1,0:T(1,128)S(1)}, u32[]{:S(2)}, u32[]{:S(2)}) async-start(s32[8,1,1024]{2,1,0:T(1,128)} %compare_select_fusion), calls=%async_computation | async-start | bytes 65536 | tf_op jit(solution)/shard_map/all_to_all | solution.py:51
  16.7 35.3 %all-to-all-start.1 = ((bf16[8,80,1024]{2,1,0:T(8,128)(2,1)}), bf16[8,80,1024]{2,1,0:T(8,128)(2,1)S(1)}, u32[]{:S(2)}, u32[]{:S(2)}) async-start(bf16[8,80,1024]{2,1,0:T(8,128)(2,1)} %fusion.9), calls=%async_computation.1 | async-start | bytes 2621440 | tf_op jit(solution)/shard_map/all_to_all | solution.py:50
where the time goes:
time: 81.2 us; the launch traced here: 80 us
  waiting for transfers between devices  29.9 us (37%)
  matrix products  22 us (27%)
  starting transfers between devices  11.8 us (15%)
  blocking collectives  11.2 us (14%)
  other arithmetic  4.13 us (5%)
  local copies, waits for them, and re-layouts  1.02 us (1%)
    all_to_all x1, waiting for transfers between devices, body(): lax.all_to_all(values, 'bev', split_axis=0, concat_axis=0, tiled=True)  29.9 us
    dot_general x1, matrix products, pool_total(): jnp.einsum('gcs,gsn->nc', values, onehot, preferred_element_type=jnp.floa...  15.9 us
    all_to_all x1, blocking collectives, body(): lax.all_to_all(rounded, 'scene', split_axis=0, concat_axis=2, tiled=True)  11.2 us
    all_to_all x1, starting transfers between devices, body(): lax.all_to_all(targets, 'bev', split_axis=0, concat_axis=0, tiled=True)  6.35 us
    all_to_all x1, starting transfers between devices, body(): lax.all_to_all(values, 'bev', split_axis=0, concat_axis=0, tiled=True)  5.43 us
    dot_general x1, matrix products, select_points(): jnp.einsum('nsk,kp->nsp', depth_hot, depth_prob, preferred_element_type=j...  3.24 us
    dot_general x1, matrix products, select_points(): jnp.einsum('nsp,cp->ncs', pixel_hot, context_map, preferred_element_type=...  2.9 us
  transfers between devices with their start and end apart: 2, of which 1 were waited for; matrix products, arithmetic and copies ran while one was open for 11% of the time, Pallas kernels for 0%

commit v1 on v0

v1 whole, which is shorter than its diff:
```python
import functools

import jax
import jax.numpy as jnp
from jax import lax
from jax.experimental import pallas as pl
from jax.experimental.pallas import tpu as pltpu
from jax.sharding import PartitionSpec as P

GRID = 128
LANES = 128
LOW = 4
MESH = pl.DeviceIdType.MESH


def kernel(strips, scenes, strip_cells, context_ref, logits_ref, count_ref, point_ref, cell_ref,
           out_ref, context_all, sent, got, prob, total, parts,
           ctx_send, ctx_recv, slot_send, slot_recv, part_send, part_recv):
    channels, pix_block = context_ref.shape
    depth_bins = logits_ref.shape[0]
    capacity = point_ref.shape[1]
    rows = capacity // LANES
    quarter = strip_cells // scenes
    sub = quarter // LOW
    me = lax.axis_index("bev")
    scene = lax.axis_index("scene")

    barrier = pltpu.get_barrier_semaphore()

    @pl.loop(1, strips)
    def _(step):
        pl.semaphore_signal(barrier, inc=1, device_id={"bev": lax.rem(me + step, strips)}, device_id_type=MESH)

    @pl.loop(1, scenes)
    def _(step):
        pl.semaphore_signal(barrier, inc=1, device_id={"scene": lax.rem(scene + step, scenes)}, device_id_type=MESH)

    logits = logits_ref[...]
    powers = jnp.exp(logits - jnp.max(logits, axis=0, keepdims=True))
    prob[...] = (powers / jnp.sum(powers, axis=0, keepdims=True)).astype(jnp.bfloat16)
    pl.semaphore_wait(barrier, strips - 1 + scenes - 1)

    def context_copy(step):
        return pltpu.make_async_remote_copy(
            src_ref=context_ref, dst_ref=context_all.at[me],
            send_sem=ctx_send.at[step], recv_sem=ctx_recv.at[me],
            device_id={"bev": lax.rem(me + step, strips)}, device_id_type=MESH)

    def slot_copy(step):
        to = lax.rem(me + step, strips)
        return pltpu.make_async_remote_copy(
            src_ref=sent.at[to], dst_ref=got.at[me],
            send_sem=slot_send.at[step], recv_sem=slot_recv.at[me],
            device_id={"bev": to}, device_id_type=MESH)

    @pl.loop(1, strips)
    def _(step):
        context_copy(step).start()

    pixel_row = lax.broadcasted_iota(jnp.int32, (pix_block, capacity), 0)
    depth_row = lax.broadcasted_iota(jnp.int32, (depth_bins, capacity), 0)
    slot_row = lax.broadcasted_iota(jnp.int32, (1, capacity), 1)

    def fill(to):
        points = point_ref[pl.ds(to, 1), :]
        live = slot_row < count_ref[0, to]
        pixel = points % pix_block
        depth = points // pix_block
        hot = jnp.where(pixel_row == pixel, 1.0, 0.0).astype(jnp.bfloat16)
        column = jnp.dot(prob[...], hot, preferred_element_type=jnp.float32)
        weight = jnp.sum(jnp.where(depth_row == depth, column, 0.0), axis=0, keepdims=True)
        weight = jnp.where(live, weight, 0.0)
        cell = jnp.where(live, cell_ref[pl.ds(to, 1), :], strip_cells)
        code = (cell * pix_block + pixel).astype(jnp.float32)
        for r in range(rows):
            sent[to, r:r + 1, :] = weight[:, r * LANES:(r + 1) * LANES]
            sent[to, rows + r:rows + r + 1, :] = code[:, r * LANES:(r + 1) * LANES]

    @pl.loop(1, strips)
    def _(step):
        fill(lax.rem(me + step, strips))
        slot_copy(step).start()

    fill(me)
    total[...] = jnp.zeros_like(total)
    high_row = lax.broadcasted_iota(jnp.int32, (scenes * sub, capacity), 0)

    def pool(features_map, slots):
        weight = jnp.concatenate([slots[r:r + 1, :] for r in range(rows)], axis=1)
        code = jnp.concatenate([slots[rows + r:rows + r + 1, :] for r in range(rows)], axis=1).astype(jnp.int32)
        pixel = code % pix_block
        cell = code // pix_block
        high = (cell // quarter) * sub + cell % sub
        low = (cell // sub) % LOW
        pixel_hot = jnp.where(pixel_row == pixel, 1.0, 0.0).astype(jnp.bfloat16)
        features = jnp.dot(features_map, pixel_hot, preferred_element_type=jnp.float32)
        values = features * weight
        spread = jnp.concatenate(
            [jnp.where(low == j, values, 0.0).astype(jnp.bfloat16) for j in range(LOW)], axis=0)
        high_hot = jnp.where(high_row == high, 1.0, 0.0).astype(jnp.bfloat16)
        total[...] += lax.dot_general(
            spread, high_hot, (((1,), (1,)), ((), ())), preferred_element_type=jnp.float32)

    pool(context_ref[...], sent[me])

    @pl.loop(1, strips)
    def _(step):
        source = lax.rem(me + strips - step, strips)
        pltpu.make_async_remote_copy(
            src_ref=context_ref, dst_ref=context_all.at[source],
            send_sem=ctx_send.at[step], recv_sem=ctx_recv.at[source],
            device_id={"bev": source}, device_id_type=MESH).wait_recv()
        pltpu.make_async_remote_copy(
            src_ref=sent.at[source], dst_ref=got.at[source],
            send_sem=slot_send.at[step], recv_sem=slot_recv.at[source],
            device_id={"bev": source}, device_id_type=MESH).wait_recv()
        pool(context_all[source], got[source])

    for q in range(scenes):
        for j in range(LOW):
            parts[q, j] = total[j * channels:(j + 1) * channels, q * sub:(q + 1) * sub].astype(jnp.bfloat16)

    def part_copy(step):
        to = lax.rem(scene + step, scenes)
        return pltpu.make_async_remote_copy(
            src_ref=parts.at[to], dst_ref=out_ref.at[:, pl.ds(pl.multiple_of(scene * channels, 16), channels), :],
            send_sem=part_send.at[step], recv_sem=part_recv.at[scene],
            device_id={"scene": to}, device_id_type=MESH)

    @pl.loop(1, scenes)
    def _(step):
        part_copy(step).start()

    out_ref[:, pl.ds(pl.multiple_of(scene * channels, 16), channels), :] = parts[scene]

    @pl.loop(1, strips)
    def _(step):
        context_copy(step).wait_send()
        slot_copy(step).wait_send()

    @pl.loop(1, scenes)
    def _(step):
        source = lax.rem(scene + scenes - step, scenes)
        pltpu.make_async_remote_copy(
            src_ref=parts.at[source],
            dst_ref=out_ref.at[:, pl.ds(pl.multiple_of(source * channels, 16), channels), :],
            send_sem=part_send.at[step], recv_sem=part_recv.at[source],
            device_id={"scene": source}, device_id_type=MESH).wait_recv()
        part_copy(step).wait_send()


def body(context, depth_logits, send_count, slot_point, slot_cell):
    strips = lax.axis_size("bev")
    scenes = lax.axis_size("scene")
    strip_cells = GRID * GRID // strips
    channels, pix_block = context.shape[1:]
    depth_bins = depth_logits.shape[1]
    capacity = slot_point.shape[3]
    quarter = strip_cells // scenes
    sub = quarter // LOW
    vmem = pl.BlockSpec(memory_space=pltpu.VMEM)
    slots = (strips, 2 * capacity // LANES, LANES)
    pooled = pl.pallas_call(
        functools.partial(kernel, strips, scenes, strip_cells),
        out_shape=jax.ShapeDtypeStruct((LOW, scenes * channels, sub), jnp.bfloat16),
        in_specs=[vmem, vmem, pl.BlockSpec(memory_space=pltpu.SMEM), vmem, vmem],
        out_specs=vmem,
        scratch_shapes=[
            pltpu.VMEM((strips, channels, pix_block), jnp.bfloat16),
            pltpu.VMEM(slots, jnp.float32),
            pltpu.VMEM(slots, jnp.float32),
            pltpu.VMEM((depth_bins, pix_block), jnp.bfloat16),
            pltpu.VMEM((LOW * channels, scenes * sub), jnp.float32),
            pltpu.VMEM((scenes, LOW, channels, sub), jnp.bfloat16),
            pltpu.SemaphoreType.DMA((strips,)),
            pltpu.SemaphoreType.DMA((strips,)),
            pltpu.SemaphoreType.DMA((strips,)),
            pltpu.SemaphoreType.DMA((strips,)),
            pltpu.SemaphoreType.DMA((scenes,)),
            pltpu.SemaphoreType.DMA((scenes,)),
        ],
        compiler_params=pltpu.CompilerParams(
            collective_id=0, has_side_effects=True, vmem_limit_bytes=48 * 1024 * 1024),
    )(context[0], depth_logits[0], send_count[0], slot_point[0, 0], slot_cell[0, 0])
    return jnp.transpose(pooled, (0, 2, 1)).reshape(quarter, scenes * channels)


def solution(mesh):
    return jax.shard_map(
        body,
        mesh=mesh,
        in_specs=(
            P("scene", None, "bev"),
            P("scene", None, "bev"),
            P("scene", "bev", None),
            P("scene", "bev", None, None),
            P("scene", "bev", None, None),
        ),
        out_specs=P(("bev", "scene"), None),
        check_vma=False,
    )
```

time: 81.2 us -> 28.8 us (0.35); the launches traced: 80 us -> 28.5 us
  waiting for transfers between devices: 29.9 us -> 0 us
  Pallas kernels: 0 us -> 23.8 us
  matrix products: 22 us -> 0 us
  starting transfers between devices: 11.8 us -> 0 us
  blocking collectives: 11.2 us -> 0 us
  other arithmetic: 4.13 us -> 0 us
  local copies, waits for them, and re-layouts: 1.02 us -> 4.61 us
    all_to_all x2 -> x0, waiting for transfers between devices: 29.9 us -> none  [the longest x1 29.9 us: body(): lax.all_to_all(values, 'bev', split_axis=0, concat_axis=0, tiled=True)]
    pallas_call x0 -> x1, Pallas kernels: none -> 23.8 us  [body(): pl.pallas_call(functools.partial(kernel, strips, scenes, strip_cells), ou...]
    dot_general x3 -> x0, matrix products: 22 us -> none  [the longest x1 15.9 us: pool_total(): jnp.einsum('gcs,gsn->nc', values, onehot, preferred_element_type=jnp.floa...]
    all_to_all x2 -> x0, starting transfers between devices: 11.8 us -> none  [the longest x1 6.35 us: body(): lax.all_to_all(targets, 'bev', split_axis=0, concat_axis=0, tiled=True)]
    all_to_all x1 -> x0, blocking collectives: 11.2 us -> none  [body(): lax.all_to_all(rounded, 'scene', split_axis=0, concat_axis=2, tiled=True)]
    unnamed x4 -> x10, local copies, waits for them, and re-layouts: 0.74 us -> 3.85 us
    select_n x2 -> x0, other arithmetic: 2.26 us -> none  [the longest x1 1.47 us: body(): targets = jnp.where(live_mask, slot_cell[0, 0], strip_cells)]
    reduce_sum x1 -> x0, other arithmetic: 0.94 us -> none  [body(): depth_prob = jax.nn.softmax(depth_logits[0], axis=0).astype(jnp.bfloat16)]
  transfers between devices with their start and end apart: 2 -> 0, of which waited for: 1 -> 0; matrix products, arithmetic and copies ran while one was open for 11% -> 0% of each run, Pallas kernels for 0% -> 0%
where the time goes in v1:
time: 28.8 us; the launch traced here: 28.5 us
  Pallas kernels  23.8 us (83%)
  local copies, waits for them, and re-layouts  4.61 us (16%)
    pallas_call x1, Pallas kernels, body(): pl.pallas_call(functools.partial(kernel, strips, scenes, strip_cells), ou...  23.8 us
    unnamed x10, local copies, waits for them, and re-layouts  3.85 us
    reshape x1, local copies, waits for them, and re-layouts, body(): return jnp.transpose(pooled, (0, 2, 1)).reshape(quarter, scenes * channels)  0.76 us

profile of v1, /device:TPU:1, one launch (start us, length us, event | category | flops | bytes accessed | tf_op | source)
XLA Modules:
  0.0 28.5 jit_solution(5914006905106724010)
XLA Ops:
  0.0 0.0 copy-start.4
  0.0 0.7 %copy-done.4 = s32[1,1,8]{2,1,0:T(1,128)S(1)} copy-done((s32[1,1,8]{2,1,0:T(1,128)S(1)}, s32[1,1,8]{2,1,0:T(1,128)}, u32[]{:S(2)}) %copy-start.4) | copy-done | bytes 56
  0.7 0.0 copy-start
  0.7 0.9 %copy-done = f32[1,112,256]{2,1,0:T(8,128)S(1)} copy-done((f32[1,112,256]{2,1,0:T(8,128)S(1)}, f32[1,112,256]{2,1,0:T(8,128)}, u32[]{:S(2)}) %copy-start) | copy-done | bytes 114712
  1.6 0.0 copy-start.1
  1.6 0.8 %copy-done.1 = bf16[1,80,256]{2,1,0:T(8,128)(2,1)S(1)} copy-done((bf16[1,80,256]{2,1,0:T(8,128)(2,1)S(1)}, bf16[1,80,256]{2,1,0:T(8,128)(2,1)}, u32[]{:S(2)}) %copy-start.1) | copy-done | bytes 40984
  2.3 0.0 copy-start.2
  2.3 0.8 %copy-done.2 = s32[1,1,8,1024]{3,2,1,0:T(8,128)S(1)} copy-done((s32[1,1,8,1024]{3,2,1,0:T(8,128)S(1)}, s32[1,1,8,1024]{3,2,1,0:T(8,128)}, u32[]{:S(2)}) %copy-start.2) | copy-done | bytes 32792
  3.1 0.0 copy-start.3
  3.1 0.8 %copy-done.3 = s32[1,1,8,1024]{3,2,1,0:T(8,128)S(1)} copy-done((s32[1,1,8,1024]{3,2,1,0:T(8,128)S(1)}, s32[1,1,8,1024]{3,2,1,0:T(8,128)}, u32[]{:S(2)}) %copy-start.3) | copy-done | bytes 32792
  3.9 23.8 %shard_map.55 = bf16[4,320,128]{2,1,0:T(8,128)(2,1)S(1)} custom-call(bf16[80,256]{1,0:T(8,128)(2,1)S(1)} %bitcast.12, f32[112,256]{1,0:T(8,128)S(1)} %bitcast.11, s32[1,8]{1,0:T(1,128)S(1)} %bitcast.15, s32[8,1024]{1,0:T(8,128)S(1)} %bitcast.13, s32[8,1024]{1,0:T(8,128)S(1)} %bitcast.14), custom_call_target="tpu_custom_call" | custom-call | tf_op jit(solution)/shard_map/pallas_call | solution.py:163
  27.7 0.8 %copy_bitcast_fusion = bf16[512,320]{0,1:T(8,128)(2,1)} fusion(bf16[4,320,128]{2,1,0:T(8,128)(2,1)S(1)} %shard_map.55), kind=kLoop, calls=%fused_computation | loop fusion | bytes 655360 | tf_op jit(solution)/shard_map/reshape | solution.py:185
Async XLA Ops:
  0.0 0.7 %copy-start.4 = (s32[1,1,8]{2,1,0:T(1,128)S(1)}, s32[1,1,8]{2,1,0:T(1,128)}, u32[]{:S(2)}) copy-start(s32[1,1,8]{2,1,0:T(1,128)} %param.7) | copy-start | bytes 100
  0.7 0.9 %copy-start = (f32[1,112,256]{2,1,0:T(8,128)S(1)}, f32[1,112,256]{2,1,0:T(8,128)}, u32[]{:S(2)}) copy-start(f32[1,112,256]{2,1,0:T(8,128)} %param.6) | copy-start | bytes 344068
  1.6 0.8 %copy-start.1 = (bf16[1,80,256]{2,1,0:T(8,128)(2,1)S(1)}, bf16[1,80,256]{2,1,0:T(8,128)(2,1)}, u32[]{:S(2)}) copy-start(bf16[1,80,256]{2,1,0:T(8,128)(2,1)} %param.5) | copy-start | bytes 122884
  2.3 0.8 %copy-start.2 = (s32[1,1,8,1024]{3,2,1,0:T(8,128)S(1)}, s32[1,1,8,1024]{3,2,1,0:T(8,128)}, u32[]{:S(2)}) copy-start(s32[1,1,8,1024]{3,2,1,0:T(8,128)} %param.8) | copy-start | bytes 98308
  3.1 0.8 %copy-start.3 = (s32[1,1,8,1024]{3,2,1,0:T(8,128)S(1)}, s32[1,1,8,1024]{3,2,1,0:T(8,128)}, u32[]{:S(2)}) copy-start(s32[1,1,8,1024]{3,2,1,0:T(8,128)} %param.9) | copy-start | bytes 98308

commit v2 on v1

v2 whole, which is shorter than its diff:
```python
import functools

import jax
import jax.numpy as jnp
from jax import lax
from jax.experimental import pallas as pl
from jax.experimental.pallas import tpu as pltpu
from jax.sharding import PartitionSpec as P

GRID = 128
LANES = 128
LOW = 4
HALVES = 2
MESH = pl.DeviceIdType.MESH


def kernel(strips, scenes, strip_cells, context_hbm, logits_hbm, count_hbm, point_hbm, cell_hbm,
           out_ref, context_ref, logits_ref, count_ref, point_ref, cell_ref,
           context_all, sent, got, prob, values_all, total, parts,
           load, ctx_send, ctx_recv, slot_send, slot_recv, part_send, part_recv):
    channels, pix_block = context_ref.shape
    depth_bins = logits_ref.shape[0]
    capacity = point_ref.shape[1]
    rows = capacity // LANES
    quarter = strip_cells // scenes
    sub = quarter // LOW
    group = scenes // HALVES
    half_rows = group * sub
    assert pix_block <= 256 and half_rows <= 256
    me = lax.axis_index("bev")
    scene = lax.axis_index("scene")

    loads = [
        pltpu.make_async_copy(src, dst, load.at[i])
        for i, (src, dst) in enumerate([
            (logits_hbm, logits_ref), (context_hbm, context_ref), (point_hbm, point_ref),
            (cell_hbm, cell_ref), (count_hbm, count_ref)])
    ]
    for copy in loads:
        copy.start()

    barrier = pltpu.get_barrier_semaphore()

    @pl.loop(1, strips)
    def _(step):
        pl.semaphore_signal(barrier, inc=1, device_id={"bev": lax.rem(me + step, strips)}, device_id_type=MESH)

    @pl.loop(1, scenes)
    def _(step):
        pl.semaphore_signal(barrier, inc=1, device_id={"scene": lax.rem(scene + step, scenes)}, device_id_type=MESH)

    loads[0].wait()
    logits = logits_ref[...]
    powers = jnp.exp(logits - jnp.max(logits, axis=0, keepdims=True))
    prob[...] = (powers / jnp.sum(powers, axis=0, keepdims=True)).astype(jnp.bfloat16)
    for copy in loads[1:]:
        copy.wait()
    pl.semaphore_wait(barrier, strips - 1 + scenes - 1)

    def context_copy(step):
        return pltpu.make_async_remote_copy(
            src_ref=context_ref, dst_ref=context_all.at[me],
            send_sem=ctx_send.at[step], recv_sem=ctx_recv.at[me],
            device_id={"bev": lax.rem(me + step, strips)}, device_id_type=MESH)

    def slot_copy(step):
        to = lax.rem(me + step, strips)
        return pltpu.make_async_remote_copy(
            src_ref=sent.at[to], dst_ref=got.at[me],
            send_sem=slot_send.at[step], recv_sem=slot_recv.at[me],
            device_id={"bev": to}, device_id_type=MESH)

    @pl.loop(1, strips)
    def _(step):
        context_copy(step).start()

    def hot_rows(count, ids):
        row = lax.broadcasted_iota(jnp.int32, (count, capacity), 0).astype(jnp.bfloat16)
        return jnp.where(row == ids.astype(jnp.bfloat16), jnp.bfloat16(1), jnp.bfloat16(0))

    depth_row = lax.broadcasted_iota(jnp.int32, (depth_bins, capacity), 0)
    slot_row = lax.broadcasted_iota(jnp.int32, (1, capacity), 1)

    def fill(to):
        points = point_ref[pl.ds(to, 1), :]
        live = slot_row < count_ref[0, to]
        pixel = points % pix_block
        depth = points // pix_block
        column = jnp.dot(prob[...], hot_rows(pix_block, pixel), preferred_element_type=jnp.float32)
        weight = jnp.sum(jnp.where(depth_row == depth, column, 0.0), axis=0, keepdims=True)
        weight = jnp.where(live, weight, 0.0)
        cell = jnp.where(live, cell_ref[pl.ds(to, 1), :], strip_cells)
        code = (cell * pix_block + pixel).astype(jnp.float32)
        for r in range(rows):
            sent[to, r:r + 1, :] = weight[:, r * LANES:(r + 1) * LANES]
            sent[to, rows + r:rows + r + 1, :] = code[:, r * LANES:(r + 1) * LANES]

    @pl.loop(1, strips)
    def _(step):
        fill(lax.rem(me + step, strips))
        slot_copy(step).start()

    fill(me)

    def line(block):
        return jnp.concatenate([block[r:r + 1, :] for r in range(rows)], axis=1)

    def scatter(half, cell, values):
        high = (cell // quarter) * sub + cell % sub - half * half_rows
        low = (cell // sub) % LOW
        spread = jnp.concatenate(
            [values * jnp.where(low == j, 1.0, 0.0).astype(jnp.bfloat16) for j in range(LOW)], axis=0)
        return lax.dot_general(
            spread, hot_rows(half_rows, high), (((1,), (1,)), ((), ())), preferred_element_type=jnp.float32)

    def form(features_map, slots, source, half):
        code = line(slots[rows:, :]).astype(jnp.int32)
        features = jnp.dot(features_map, hot_rows(pix_block, code % pix_block), preferred_element_type=jnp.float32)
        values = (features * line(slots[:rows, :])).astype(jnp.bfloat16)
        values_all[source] = values
        return scatter(half, code // pix_block, values)

    near = scene // group
    far = lax.rem(near + 1, HALVES)
    total[...] = form(context_ref[...], sent[me], me, far)

    @pl.loop(1, strips)
    def _(step):
        source = lax.rem(me + strips - step, strips)
        pltpu.make_async_remote_copy(
            src_ref=context_ref, dst_ref=context_all.at[source],
            send_sem=ctx_send.at[step], recv_sem=ctx_recv.at[source],
            device_id={"bev": source}, device_id_type=MESH).wait_recv()
        pltpu.make_async_remote_copy(
            src_ref=sent.at[source], dst_ref=got.at[source],
            send_sem=slot_send.at[step], recv_sem=slot_recv.at[source],
            device_id={"bev": source}, device_id_type=MESH).wait_recv()
        total[...] += form(context_all[source], got[source], source, far)

    def pack(half):
        for q in range(group):
            for j in range(LOW):
                parts[half * group + q, j] = total[
                    j * channels:(j + 1) * channels, q * sub:(q + 1) * sub].astype(jnp.bfloat16)

    def place(source):
        return out_ref.at[:, pl.ds(pl.multiple_of(source * channels, 16), channels), :]

    def part_copy(to):
        return pltpu.make_async_remote_copy(
            src_ref=parts.at[to], dst_ref=place(scene),
            send_sem=part_send.at[to], recv_sem=part_recv.at[scene],
            device_id={"scene": to}, device_id_type=MESH)

    pack(far)
    for q in range(group):
        part_copy(far * group + q).start()

    total[...] = scatter(near, line(sent[me][rows:, :]).astype(jnp.int32) // pix_block, values_all[me])

    @pl.loop(1, strips)
    def _(step):
        source = lax.rem(me + strips - step, strips)
        total[...] += scatter(near, line(got[source][rows:, :]).astype(jnp.int32) // pix_block, values_all[source])

    pack(near)
    others = [near * group + lax.rem(scene + o, group) for o in range(1, group)]
    for to in others:
        part_copy(to).start()
    out_ref[:, pl.ds(pl.multiple_of(scene * channels, 16), channels), :] = parts[scene]

    @pl.loop(1, strips)
    def _(step):
        context_copy(step).wait_send()
        slot_copy(step).wait_send()

    for to in [far * group + q for q in range(group)] + others:
        part_copy(to).wait_send()
        pltpu.make_async_remote_copy(
            src_ref=parts.at[to], dst_ref=place(to),
            send_sem=part_send.at[to], recv_sem=part_recv.at[to],
            device_id={"scene": to}, device_id_type=MESH).wait_recv()


def body(context, depth_logits, send_count, slot_point, slot_cell):
    strips = lax.axis_size("bev")
    scenes = lax.axis_size("scene")
    strip_cells = GRID * GRID // strips
    channels, pix_block = context.shape[1:]
    depth_bins = depth_logits.shape[1]
    capacity = slot_point.shape[3]
    quarter = strip_cells // scenes
    sub = quarter // LOW
    hbm = pl.BlockSpec(memory_space=pltpu.HBM)
    slots = (strips, 2 * capacity // LANES, LANES)
    pooled = pl.pallas_call(
        functools.partial(kernel, strips, scenes, strip_cells),
        out_shape=jax.ShapeDtypeStruct((LOW, scenes * channels, sub), jnp.bfloat16),
        in_specs=[hbm] * 5,
        out_specs=pl.BlockSpec(memory_space=pltpu.VMEM),
        scratch_shapes=[
            pltpu.VMEM((channels, pix_block), jnp.bfloat16),
            pltpu.VMEM((depth_bins, pix_block), jnp.float32),
            pltpu.SMEM((1, strips), jnp.int32),
            pltpu.VMEM((strips, capacity), jnp.int32),
            pltpu.VMEM((strips, capacity), jnp.int32),
            pltpu.VMEM((strips, channels, pix_block), jnp.bfloat16),
            pltpu.VMEM(slots, jnp.float32),
            pltpu.VMEM(slots, jnp.float32),
            pltpu.VMEM((depth_bins, pix_block), jnp.bfloat16),
            pltpu.VMEM((strips, channels, capacity), jnp.bfloat16),
            pltpu.VMEM((LOW * channels, scenes // HALVES * sub), jnp.float32),
            pltpu.VMEM((scenes, LOW, channels, sub), jnp.bfloat16),
            pltpu.SemaphoreType.DMA((5,)),
            pltpu.SemaphoreType.DMA((strips,)),
            pltpu.SemaphoreType.DMA((strips,)),
            pltpu.SemaphoreType.DMA((strips,)),
            pltpu.SemaphoreType.DMA((strips,)),
            pltpu.SemaphoreType.DMA((scenes,)),
            pltpu.SemaphoreType.DMA((scenes,)),
        ],
        compiler_params=pltpu.CompilerParams(
            collective_id=0, has_side_effects=True, vmem_limit_bytes=64 * 1024 * 1024),
    )(context[0], depth_logits[0], send_count[0], slot_point[0, 0], slot_cell[0, 0])
    return jnp.transpose(pooled, (0, 2, 1)).reshape(quarter, scenes * channels)


def solution(mesh):
    return jax.shard_map(
        body,
        mesh=mesh,
        in_specs=(
            P("scene", None, "bev"),
            P("scene", None, "bev"),
            P("scene", "bev", None),
            P("scene", "bev", None, None),
            P("scene", "bev", None, None),
        ),
        out_specs=P(("bev", "scene"), None),
        check_vma=False,
    )
```

time: 28.8 us -> 25.6 us (0.89)
  local copies, waits for them, and re-layouts: 4.61 us -> 1.73 us
    unnamed x10 -> x0, local copies, waits for them, and re-layouts: 3.85 us -> none
    reshape x1, local copies, waits for them, and re-layouts: 0.76 us -> 1.73 us  [body(): return jnp.transpose(pooled, (0, 2, 1)).reshape(quarter, scenes * channels)]
where the time goes in v2:
time: 25.6 us; the launch traced here: 25.4 us
  Pallas kernels  23.6 us (92%)
  local copies, waits for them, and re-layouts  1.73 us (7%)
    pallas_call x1, Pallas kernels, body(): pl.pallas_call(functools.partial(kernel, strips, scenes, strip_cells), ou...  23.6 us
    reshape x1, local copies, waits for them, and re-layouts, body(): return jnp.transpose(pooled, (0, 2, 1)).reshape(quarter, scenes * channels)  1.73 us

profile of v2, /device:TPU:1, one launch (start us, length us, event | category | flops | bytes accessed | tf_op | source)
XLA Modules:
  0.0 25.4 jit_solution(5669369333992356039)
XLA Ops:
  0.0 23.6 %shard_map.55 = bf16[4,320,128]{2,1,0:T(8,128)(2,1)} custom-call(bf16[80,256]{1,0:T(8,128)(2,1)} %bitcast.12, f32[112,256]{1,0:T(8,128)} %bitcast.11, s32[1,8]{1,0:T(1,128)} %bitcast.15, s32[8,1024]{1,0:T(8,128)} %bitcast.13, s32[8,1024]{1,0:T(8,128)} %bitcast.14), custom_call_target="tpu_custom_call" | custom-call | tf_op jit(solution)/shard_map/pallas_call | solution.py:196
  23.6 1.7 %copy_bitcast_fusion = bf16[512,320]{0,1:T(8,128)(2,1)} fusion(bf16[4,320,128]{2,1,0:T(8,128)(2,1)} %shard_map.55), kind=kLoop, calls=%fused_computation | loop fusion | bytes 655360 | tf_op jit(solution)/shard_map/reshape | solution.py:225

commit v3 on v2

--- a/solution.py
+++ b/solution.py
@@ -16,7 +16,7 @@
 
 def kernel(strips, scenes, strip_cells, context_hbm, logits_hbm, count_hbm, point_hbm, cell_hbm,
            out_ref, context_ref, logits_ref, count_ref, point_ref, cell_ref,
-           context_all, sent, got, prob, values_all, total, parts,
+           context_all, sent, got, prob, row_ids, values_all, total, parts,
            load, ctx_send, ctx_recv, slot_send, slot_recv, part_send, part_recv):
     channels, pix_block = context_ref.shape
     depth_bins = logits_ref.shape[0]
@@ -57,31 +57,66 @@
         copy.wait()
     pl.semaphore_wait(barrier, strips - 1 + scenes - 1)
 
-    def context_copy(step):
+    pair = me + 1 - 2 * lax.rem(me, 2)
+    half_strips = strips // 2
+
+    def target(item):
+        start = jnp.where(item < half_strips, me, pair)
+        return lax.rem(start + 2 * lax.rem(item, half_strips), strips)
+
+    def origin(item):
+        start = jnp.where(item < half_strips, me, pair)
+        return lax.rem(start + strips - 2 * lax.rem(item, half_strips), strips)
+
+    def own_context(item):
         return pltpu.make_async_remote_copy(
             src_ref=context_ref, dst_ref=context_all.at[me],
-            send_sem=ctx_send.at[step], recv_sem=ctx_recv.at[me],
-            device_id={"bev": lax.rem(me + step, strips)}, device_id_type=MESH)
-
-    def slot_copy(step):
-        to = lax.rem(me + step, strips)
+            send_sem=ctx_send.at[item], recv_sem=ctx_recv.at[me],
+            device_id={"bev": target(item)}, device_id_type=MESH)
+
+    def passed_context(item):
+        source = origin(item)
+        return pltpu.make_async_remote_copy(
+            src_ref=context_all.at[source], dst_ref=context_all.at[source],
+            send_sem=ctx_send.at[half_strips + item], recv_sem=ctx_recv.at[source],
+            device_id={"bev": pair}, device_id_type=MESH)
+
+    def context_arrived(item):
+        source = origin(item)
+        pltpu.make_async_remote_copy(
+            src_ref=context_ref, dst_ref=context_all.at[source],
+            send_sem=ctx_send.at[item], recv_sem=ctx_recv.at[source],
+            device_id={"bev": source}, device_id_type=MESH).wait_recv()
+
+    def slot_copy(item):
+        to = target(item)
         return pltpu.make_async_remote_copy(
             src_ref=sent.at[to], dst_ref=got.at[me],
-            send_sem=slot_send.at[step], recv_sem=slot_recv.at[me],
+            send_sem=slot_send.at[item], recv_sem=slot_recv.at[me],
             device_id={"bev": to}, device_id_type=MESH)
 
-    @pl.loop(1, strips)
-    def _(step):
-        context_copy(step).start()
+    def slots_arrived(item):
+        source = origin(item)
+        pltpu.make_async_remote_copy(
+            src_ref=sent.at[source], dst_ref=got.at[source],
+            send_sem=slot_send.at[item], recv_sem=slot_recv.at[source],
+            device_id={"bev": source}, device_id_type=MESH).wait_recv()
+
+    @pl.loop(1, half_strips + 1)
+    def _(item):
+        own_context(item).start()
+
+    context_all[me] = context_ref[...]
+    row_ids[...] = lax.broadcasted_iota(jnp.int32, row_ids.shape, 0).astype(jnp.bfloat16)
 
     def hot_rows(count, ids):
-        row = lax.broadcasted_iota(jnp.int32, (count, capacity), 0).astype(jnp.bfloat16)
+        row = jnp.concatenate([row_ids[:count, :]] * (ids.shape[1] // LANES), axis=1)
         return jnp.where(row == ids.astype(jnp.bfloat16), jnp.bfloat16(1), jnp.bfloat16(0))
 
     depth_row = lax.broadcasted_iota(jnp.int32, (depth_bins, capacity), 0)
     slot_row = lax.broadcasted_iota(jnp.int32, (1, capacity), 1)
 
-    def fill(to):
+    def fill(to, slots, place):
         points = point_ref[pl.ds(to, 1), :]
         live = slot_row < count_ref[0, to]
         pixel = points % pix_block
@@ -92,15 +127,32 @@
         cell = jnp.where(live, cell_ref[pl.ds(to, 1), :], strip_cells)
         code = (cell * pix_block + pixel).astype(jnp.float32)
         for r in range(rows):
-            sent[to, r:r + 1, :] = weight[:, r * LANES:(r + 1) * LANES]
-            sent[to, rows + r:rows + r + 1, :] = code[:, r * LANES:(r + 1) * LANES]
-
-    @pl.loop(1, strips)
-    def _(step):
-        fill(lax.rem(me + step, strips))
-        slot_copy(step).start()
-
-    fill(me)
+            slots[place, r:r + 1, :] = weight[:, r * LANES:(r + 1) * LANES]
+            slots[place, rows + r:rows + r + 1, :] = code[:, r * LANES:(r + 1) * LANES]
+
+    def fill_two(group):
+        for item in (2 * group + 1, 2 * group + 2):
+            fill(target(item), sent, target(item))
+        for item in (2 * group + 1, 2 * group + 2):
+            slot_copy(item).start()
+
+    def pass_on(item):
+        context_arrived(item)
+        passed_context(item).start()
+
+    fill_two(0)
+    fill_two(1)
+
+    @pl.loop(1, half_strips - 2)
+    def _(item):
+        pass_on(item)
+        fill_two(item + 1)
+
+    pass_on(half_strips - 2)
+    fill(target(strips - 1), sent, target(strips - 1))
+    slot_copy(strips - 1).start()
+    fill(me, got, me)
+    pass_on(half_strips - 1)
 
     def line(block):
         return jnp.concatenate([block[r:r + 1, :] for r in range(rows)], axis=1)
@@ -113,38 +165,49 @@
         return lax.dot_general(
             spread, hot_rows(half_rows, high), (((1,), (1,)), ((), ())), preferred_element_type=jnp.float32)
 
-    def form(features_map, slots, source, half):
-        code = line(slots[rows:, :]).astype(jnp.int32)
-        features = jnp.dot(features_map, hot_rows(pix_block, code % pix_block), preferred_element_type=jnp.float32)
-        values = (features * line(slots[:rows, :])).astype(jnp.bfloat16)
+    def codes(source):
+        return line(got[source][rows:, :]).astype(jnp.int32)
+
+    def form(source):
+        code = codes(source)
+        features = jnp.dot(
+            context_all[source], hot_rows(pix_block, code % pix_block), preferred_element_type=jnp.float32)
+        values = (features * line(got[source][:rows, :])).astype(jnp.bfloat16)
         values_all[source] = values
-        return scatter(half, code // pix_block, values)
+        return code // pix_block, values
 
     near = scene // group
     far = lax.rem(near + 1, HALVES)
-    total[...] = form(context_ref[...], sent[me], me, far)
-
-    @pl.loop(1, strips)
-    def _(step):
-        source = lax.rem(me + strips - step, strips)
-        pltpu.make_async_remote_copy(
-            src_ref=context_ref, dst_ref=context_all.at[source],
-            send_sem=ctx_send.at[step], recv_sem=ctx_recv.at[source],
-            device_id={"bev": source}, device_id_type=MESH).wait_recv()
-        pltpu.make_async_remote_copy(
-            src_ref=sent.at[source], dst_ref=got.at[source],
-            send_sem=slot_send.at[step], recv_sem=slot_recv.at[source],
-            device_id={"bev": source}, device_id_type=MESH).wait_recv()
-        total[...] += form(context_all[source], got[source], source, far)
+
+    def form_two(first):
+        made = [form(origin(item)) for item in (first, first + 1)]
+        return scatter(far, jnp.concatenate([cell for cell, _ in made], axis=1),
+                       jnp.concatenate([values for _, values in made], axis=1))
+
+    slots_arrived(1)
+    total[...] = form_two(0)
+
+    @pl.loop(1, half_strips // 2)
+    def _(step):
+        slots_arrived(2 * step)
+        slots_arrived(2 * step + 1)
+        total[...] += form_two(2 * step)
+
+    @pl.loop(half_strips // 2, half_strips)
+    def _(step):
+        for item in (2 * step, 2 * step + 1):
+            slots_arrived(item)
+            context_arrived(item)
+        total[...] += form_two(2 * step)
 
     def pack(half):
         for q in range(group):
             for j in range(LOW):
-                parts[half * group + q, j] = total[
+                parts[half * group + q, :, j * sub:(j + 1) * sub] = total[
                     j * channels:(j + 1) * channels, q * sub:(q + 1) * sub].astype(jnp.bfloat16)
 
     def place(source):
-        return out_ref.at[:, pl.ds(pl.multiple_of(source * channels, 16), channels), :]
+        return out_ref.at[pl.ds(pl.multiple_of(source * channels, 16), channels), :]
 
     def part_copy(to):
         return pltpu.make_async_remote_copy(
@@ -156,23 +219,34 @@
     for q in range(group):
         part_copy(far * group + q).start()
 
-    total[...] = scatter(near, line(sent[me][rows:, :]).astype(jnp.int32) // pix_block, values_all[me])
-
-    @pl.loop(1, strips)
-    def _(step):
-        source = lax.rem(me + strips - step, strips)
-        total[...] += scatter(near, line(got[source][rows:, :]).astype(jnp.int32) // pix_block, values_all[source])
+    def again(first):
+        sources = [2 * first, 2 * first + 1]
+        return scatter(near, jnp.concatenate([codes(source) // pix_block for source in sources], axis=1),
+                       jnp.concatenate([values_all[source] for source in sources], axis=1))
+
+    total[...] = again(0)
+
+    @pl.loop(1, half_strips)
+    def _(step):
+        total[...] += again(step)
 
     pack(near)
     others = [near * group + lax.rem(scene + o, group) for o in range(1, group)]
     for to in others:
         part_copy(to).start()
-    out_ref[:, pl.ds(pl.multiple_of(scene * channels, 16), channels), :] = parts[scene]
+    out_ref[pl.ds(pl.multiple_of(scene * channels, 16), channels), :] = parts[scene]
 
     @pl.loop(1, strips)
     def _(step):
-        context_copy(step).wait_send()
         slot_copy(step).wait_send()
+
+    @pl.loop(1, half_strips + 1)
+    def _(item):
+        own_context(item).wait_send()
+
+    @pl.loop(1, half_strips)
+    def _(item):
+        passed_context(item).wait_send()
 
     for to in [far * group + q for q in range(group)] + others:
         part_copy(to).wait_send()
@@ -195,7 +269,7 @@
     slots = (strips, 2 * capacity // LANES, LANES)
     pooled = pl.pallas_call(
         functools.partial(kernel, strips, scenes, strip_cells),
-        out_shape=jax.ShapeDtypeStruct((LOW, scenes * channels, sub), jnp.bfloat16),
+        out_shape=jax.ShapeDtypeStruct((scenes * channels, quarter), jnp.bfloat16),
         in_specs=[hbm] * 5,
         out_specs=pl.BlockSpec(memory_space=pltpu.VMEM),
         scratch_shapes=[
@@ -208,9 +282,10 @@
             pltpu.VMEM(slots, jnp.float32),
             pltpu.VMEM(slots, jnp.float32),
             pltpu.VMEM((depth_bins, pix_block), jnp.bfloat16),
+            pltpu.VMEM((256, LANES), jnp.bfloat16),
             pltpu.VMEM((strips, channels, capacity), jnp.bfloat16),
             pltpu.VMEM((LOW * channels, scenes // HALVES * sub), jnp.float32),
-            pltpu.VMEM((scenes, LOW, channels, sub), jnp.bfloat16),
+            pltpu.VMEM((scenes, channels, quarter), jnp.bfloat16),
             pltpu.SemaphoreType.DMA((5,)),
             pltpu.SemaphoreType.DMA((strips,)),
             pltpu.SemaphoreType.DMA((strips,)),
@@ -222,7 +297,7 @@
         compiler_params=pltpu.CompilerParams(
             collective_id=0, has_side_effects=True, vmem_limit_bytes=64 * 1024 * 1024),
     )(context[0], depth_logits[0], send_count[0], slot_point[0, 0], slot_cell[0, 0])
-    return jnp.transpose(pooled, (0, 2, 1)).reshape(quarter, scenes * channels)
+    return jnp.transpose(pooled)
 
 
 def solution(mesh):

time: 25.6 us -> 21.8 us (0.85)
  Pallas kernels: 23.6 us -> 20 us
    pallas_call x1, Pallas kernels: 23.6 us -> 20 us  [body(): pl.pallas_call(functools.partial(kernel, strips, scenes, strip_cells), ou...]
    reshape x1 -> x0, local copies, waits for them, and re-layouts: 1.73 us -> none  [body(): return jnp.transpose(pooled, (0, 2, 1)).reshape(quarter, scenes * channels)]
    unnamed x0 -> x1, local copies, waits for them, and re-layouts: none -> 1.72 us
where the time goes in v3:
time: 21.8 us; the launch traced here: 21.7 us
  Pallas kernels  20 us (92%)
  local copies, waits for them, and re-layouts  1.72 us (8%)
    pallas_call x1, Pallas kernels, body(): pl.pallas_call(functools.partial(kernel, strips, scenes, strip_cells), ou...  20 us
    unnamed x1, local copies, waits for them, and re-layouts  1.72 us

profile of v3, /device:TPU:1, one launch (start us, length us, event | category | flops | bytes accessed | tf_op | source)
XLA Modules:
  0.0 21.7 jit_solution(17065229628087676066)
XLA Ops:
  0.0 20.0 %shard_map.55 = bf16[320,512]{1,0:T(8,128)(2,1)} custom-call(bf16[80,256]{1,0:T(8,128)(2,1)} %bitcast.8, f32[112,256]{1,0:T(8,128)} %bitcast.7, s32[1,8]{1,0:T(1,128)} %bitcast.11, s32[8,1024]{1,0:T(8,128)} %bitcast.9, s32[8,1024]{1,0:T(8,128)} %bitcast.10), custom_call_target="tpu_custom_call" | custom-call | tf_op jit(solution)/shard_map/pallas_call | solution.py:270
  20.0 1.7 %copy.7 = bf16[512,320]{0,1:T(8,128)(2,1)} copy(bf16[512,320]{0,1:T(8,128)(2,1)} %bitcast.6) | data formatting | bytes 655360

commit v4 on v3

--- a/solution.py
+++ b/solution.py
@@ -49,63 +49,63 @@
     def _(step):
         pl.semaphore_signal(barrier, inc=1, device_id={"scene": lax.rem(scene + step, scenes)}, device_id_type=MESH)
 
+    pl.semaphore_wait(barrier, strips - 1 + scenes - 1)
+
+    pair = me + 1 - 2 * lax.rem(me, 2)
+    half_strips = strips // 2
+
+    def target(item):
+        start = jnp.where(item < half_strips, me, pair)
+        return lax.rem(start + 2 * lax.rem(item, half_strips), strips)
+
+    def origin(item):
+        start = jnp.where(item < half_strips, me, pair)
+        return lax.rem(start + strips - 2 * lax.rem(item, half_strips), strips)
+
+    def own_context(item):
+        return pltpu.make_async_remote_copy(
+            src_ref=context_hbm, dst_ref=context_all.at[me],
+            send_sem=ctx_send.at[item], recv_sem=ctx_recv.at[me],
+            device_id={"bev": target(item)}, device_id_type=MESH)
+
+    def passed_context(item):
+        source = origin(item)
+        return pltpu.make_async_remote_copy(
+            src_ref=context_all.at[source], dst_ref=context_all.at[source],
+            send_sem=ctx_send.at[half_strips + item], recv_sem=ctx_recv.at[source],
+            device_id={"bev": pair}, device_id_type=MESH)
+
+    def context_arrived(item):
+        source = origin(item)
+        pltpu.make_async_remote_copy(
+            src_ref=context_ref, dst_ref=context_all.at[source],
+            send_sem=ctx_send.at[item], recv_sem=ctx_recv.at[source],
+            device_id={"bev": source}, device_id_type=MESH).wait_recv()
+
+    def slot_copy(item):
+        to = target(item)
+        return pltpu.make_async_remote_copy(
+            src_ref=sent.at[to], dst_ref=got.at[me],
+            send_sem=slot_send.at[item], recv_sem=slot_recv.at[me],
+            device_id={"bev": to}, device_id_type=MESH)
+
+    def slots_arrived(item):
+        source = origin(item)
+        pltpu.make_async_remote_copy(
+            src_ref=sent.at[source], dst_ref=got.at[source],
+            send_sem=slot_send.at[item], recv_sem=slot_recv.at[source],
+            device_id={"bev": source}, device_id_type=MESH).wait_recv()
+
+    @pl.loop(1, half_strips + 1)
+    def _(item):
+        own_context(item).start()
+
     loads[0].wait()
     logits = logits_ref[...]
     powers = jnp.exp(logits - jnp.max(logits, axis=0, keepdims=True))
     prob[...] = (powers / jnp.sum(powers, axis=0, keepdims=True)).astype(jnp.bfloat16)
     for copy in loads[1:]:
         copy.wait()
-    pl.semaphore_wait(barrier, strips - 1 + scenes - 1)
-
-    pair = me + 1 - 2 * lax.rem(me, 2)
-    half_strips = strips // 2
-
-    def target(item):
-        start = jnp.where(item < half_strips, me, pair)
-        return lax.rem(start + 2 * lax.rem(item, half_strips), strips)
-
-    def origin(item):
-        start = jnp.where(item < half_strips, me, pair)
-        return lax.rem(start + strips - 2 * lax.rem(item, half_strips), strips)
-
-    def own_context(item):
-        return pltpu.make_async_remote_copy(
-            src_ref=context_ref, dst_ref=context_all.at[me],
-            send_sem=ctx_send.at[item], recv_sem=ctx_recv.at[me],
-            device_id={"bev": target(item)}, device_id_type=MESH)
-
-    def passed_context(item):
-        source = origin(item)
-        return pltpu.make_async_remote_copy(
-            src_ref=context_all.at[source], dst_ref=context_all.at[source],
-            send_sem=ctx_send.at[half_strips + item], recv_sem=ctx_recv.at[source],
-            device_id={"bev": pair}, device_id_type=MESH)
-
-    def context_arrived(item):
-        source = origin(item)
-        pltpu.make_async_remote_copy(
-            src_ref=context_ref, dst_ref=context_all.at[source],
-            send_sem=ctx_send.at[item], recv_sem=ctx_recv.at[source],
-            device_id={"bev": source}, device_id_type=MESH).wait_recv()
-
-    def slot_copy(item):
-        to = target(item)
-        return pltpu.make_async_remote_copy(
-            src_ref=sent.at[to], dst_ref=got.at[me],
-            send_sem=slot_send.at[item], recv_sem=slot_recv.at[me],
-            device_id={"bev": to}, device_id_type=MESH)
-
-    def slots_arrived(item):
-        source = origin(item)
-        pltpu.make_async_remote_copy(
-            src_ref=sent.at[source], dst_ref=got.at[source],
-            send_sem=slot_send.at[item], recv_sem=slot_recv.at[source],
-            device_id={"bev": source}, device_id_type=MESH).wait_recv()
-
-    @pl.loop(1, half_strips + 1)
-    def _(item):
-        own_context(item).start()
-
     context_all[me] = context_ref[...]
     row_ids[...] = lax.broadcasted_iota(jnp.int32, row_ids.shape, 0).astype(jnp.bfloat16)
 
@@ -269,7 +269,7 @@
     slots = (strips, 2 * capacity // LANES, LANES)
     pooled = pl.pallas_call(
         functools.partial(kernel, strips, scenes, strip_cells),
-        out_shape=jax.ShapeDtypeStruct((scenes * channels, quarter), jnp.bfloat16),
+        out_shape=pltpu.VMEM((scenes * channels, quarter), jnp.bfloat16),
         in_specs=[hbm] * 5,
         out_specs=pl.BlockSpec(memory_space=pltpu.VMEM),
         scratch_shapes=[
@@ -295,7 +295,7 @@
             pltpu.SemaphoreType.DMA((scenes,)),
         ],
         compiler_params=pltpu.CompilerParams(
-            collective_id=0, has_side_effects=True, vmem_limit_bytes=64 * 1024 * 1024),
+            collective_id=0, has_side_effects=True, vmem_limit_bytes=63 * 1024 * 1024),
     )(context[0], depth_logits[0], send_count[0], slot_point[0, 0], slot_cell[0, 0])
     return jnp.transpose(pooled)
 

time: 21.8 us -> 20.3 us (0.931)
  local copies, waits for them, and re-layouts: 1.72 us -> 0.73 us
  Pallas kernels: 20 us -> 19.5 us
    unnamed x1, local copies, waits for them, and re-layouts: 1.72 us -> 0.73 us
    pallas_call x1, Pallas kernels: 20 us -> 19.5 us  [body(): pl.pallas_call(functools.partial(kernel, strips, scenes, strip_cells), ou...]
where the time goes in v4:
time: 20.3 us; the launch traced here: 20.2 us
  Pallas kernels  19.5 us (96%)
  local copies, waits for them, and re-layouts  0.73 us (4%)
    pallas_call x1, Pallas kernels, body(): pl.pallas_call(functools.partial(kernel, strips, scenes, strip_cells), ou...  19.5 us
    unnamed x1, local copies, waits for them, and re-layouts  0.73 us

profile of v4, /device:TPU:1, one launch (start us, length us, event | category | flops | bytes accessed | tf_op | source)
XLA Modules:
  0.0 20.2 jit_solution(6773675957834015310)
XLA Ops:
  0.0 19.5 %shard_map.55 = bf16[320,512]{1,0:T(8,128)(2,1)S(1)} custom-call(bf16[80,256]{1,0:T(8,128)(2,1)} %bitcast.8, f32[112,256]{1,0:T(8,128)} %bitcast.7, s32[1,8]{1,0:T(1,128)} %bitcast.11, s32[8,1024]{1,0:T(8,128)} %bitcast.9, s32[8,1024]{1,0:T(8,128)} %bitcast.10), custom_call_target="tpu_custom_call" | custom-call | tf_op jit(solution)/shard_map/pallas_call | solution.py:270
  19.5 0.7 %copy.7 = bf16[512,320]{0,1:T(8,128)(2,1)} copy(bf16[512,320]{0,1:T(8,128)(2,1)S(1)} %bitcast.6) | data formatting | bytes 655360

commit v5 on v4

--- a/solution.py
+++ b/solution.py
@@ -14,8 +14,13 @@
 MESH = pl.DeviceIdType.MESH
 
 
+def log2(size):
+    assert size & (size - 1) == 0
+    return size.bit_length() - 1
+
+
 def kernel(strips, scenes, strip_cells, context_hbm, logits_hbm, count_hbm, point_hbm, cell_hbm,
-           out_ref, context_ref, logits_ref, count_ref, point_ref, cell_ref,
+           out_ref, context_ref, logits_ref, count_ref, point_ref, cell_ref, depth_table, code_table,
            context_all, sent, got, prob, row_ids, values_all, total, parts,
            load, ctx_send, ctx_recv, slot_send, slot_recv, part_send, part_recv):
     channels, pix_block = context_ref.shape
@@ -113,19 +118,25 @@
         row = jnp.concatenate([row_ids[:count, :]] * (ids.shape[1] // LANES), axis=1)
         return jnp.where(row == ids.astype(jnp.bfloat16), jnp.bfloat16(1), jnp.bfloat16(0))
 
+    points = point_ref[...]
+    target_row = lax.broadcasted_iota(jnp.int32, points.shape, 0)
+    counts = jnp.zeros_like(points)
+    for d in range(strips):
+        counts = jnp.where(target_row == d, count_ref[0, d], counts)
+    live = lax.broadcasted_iota(jnp.int32, points.shape, 1) < counts
+    pixels = points & (pix_block - 1)
+    cells = jnp.where(live, cell_ref[...], strip_cells)
+    point_ref[...] = pixels
+    depth_table[...] = jnp.where(live, points >> log2(pix_block), depth_bins)
+    code_table[...] = ((cells << log2(pix_block)) + pixels).astype(jnp.float32)
     depth_row = lax.broadcasted_iota(jnp.int32, (depth_bins, capacity), 0)
-    slot_row = lax.broadcasted_iota(jnp.int32, (1, capacity), 1)
 
     def fill(to, slots, place):
-        points = point_ref[pl.ds(to, 1), :]
-        live = slot_row < count_ref[0, to]
-        pixel = points % pix_block
-        depth = points // pix_block
-        column = jnp.dot(prob[...], hot_rows(pix_block, pixel), preferred_element_type=jnp.float32)
+        column = jnp.dot(prob[...], hot_rows(pix_block, point_ref[pl.ds(to, 1), :]),
+                         preferred_element_type=jnp.float32)
+        depth = depth_table[pl.ds(to, 1), :]
         weight = jnp.sum(jnp.where(depth_row == depth, column, 0.0), axis=0, keepdims=True)
-        weight = jnp.where(live, weight, 0.0)
-        cell = jnp.where(live, cell_ref[pl.ds(to, 1), :], strip_cells)
-        code = (cell * pix_block + pixel).astype(jnp.float32)
+        code = code_table[pl.ds(to, 1), :]
         for r in range(rows):
             slots[place, r:r + 1, :] = weight[:, r * LANES:(r + 1) * LANES]
             slots[place, rows + r:rows + r + 1, :] = code[:, r * LANES:(r + 1) * LANES]
@@ -157,32 +168,36 @@
     def line(block):
         return jnp.concatenate([block[r:r + 1, :] for r in range(rows)], axis=1)
 
-    def scatter(half, cell, values):
-        high = (cell // quarter) * sub + cell % sub - half * half_rows
-        low = (cell // sub) % LOW
+    def decode(source):
+        code = got[source][rows:, :].astype(jnp.int32)
+        return code & (pix_block - 1), code >> log2(pix_block)
+
+    def scatter(half, cells, values):
+        high = [((cell >> log2(quarter)) << log2(sub)) + (cell & (sub - 1)) - half * half_rows for cell in cells]
+        low = [(cell >> log2(sub)) & (LOW - 1) for cell in cells]
+        high = jnp.concatenate([line(block) for block in high], axis=1)
+        low = jnp.concatenate([line(block) for block in low], axis=1).astype(jnp.bfloat16)
+        values = jnp.concatenate(values, axis=1)
+        low = jnp.broadcast_to(low, values.shape)
         spread = jnp.concatenate(
-            [values * jnp.where(low == j, 1.0, 0.0).astype(jnp.bfloat16) for j in range(LOW)], axis=0)
+            [jnp.where(low == jnp.bfloat16(j), values, jnp.bfloat16(0)) for j in range(LOW)], axis=0)
         return lax.dot_general(
             spread, hot_rows(half_rows, high), (((1,), (1,)), ((), ())), preferred_element_type=jnp.float32)
 
-    def codes(source):
-        return line(got[source][rows:, :]).astype(jnp.int32)
-
     def form(source):
-        code = codes(source)
+        pixel, cell = decode(source)
         features = jnp.dot(
-            context_all[source], hot_rows(pix_block, code % pix_block), preferred_element_type=jnp.float32)
+            context_all[source], hot_rows(pix_block, line(pixel)), preferred_element_type=jnp.float32)
         values = (features * line(got[source][:rows, :])).astype(jnp.bfloat16)
         values_all[source] = values
-        return code // pix_block, values
+        return cell, values
 
     near = scene // group
     far = lax.rem(near + 1, HALVES)
 
     def form_two(first):
         made = [form(origin(item)) for item in (first, first + 1)]
-        return scatter(far, jnp.concatenate([cell for cell, _ in made], axis=1),
-                       jnp.concatenate([values for _, values in made], axis=1))
+        return scatter(far, [cell for cell, _ in made], [values for _, values in made])
 
     slots_arrived(1)
     total[...] = form_two(0)
@@ -221,8 +236,7 @@
 
     def again(first):
         sources = [2 * first, 2 * first + 1]
-        return scatter(near, jnp.concatenate([codes(source) // pix_block for source in sources], axis=1),
-                       jnp.concatenate([values_all[source] for source in sources], axis=1))
+        return scatter(near, [decode(source)[1] for source in sources], [values_all[source] for source in sources])
 
     total[...] = again(0)
 
@@ -278,6 +292,8 @@
             pltpu.SMEM((1, strips), jnp.int32),
             pltpu.VMEM((strips, capacity), jnp.int32),
             pltpu.VMEM((strips, capacity), jnp.int32),
+            pltpu.VMEM((strips, capacity), jnp.int32),
+            pltpu.VMEM((strips, capacity), jnp.float32),
             pltpu.VMEM((strips, channels, pix_block), jnp.bfloat16),
             pltpu.VMEM(slots, jnp.float32),
             pltpu.VMEM(slots, jnp.float32),

time: 20.3 us -> 20.3 us (level)
  no operation moved by 1% of the time
where the time goes in v5:
time: 20.3 us; the launch traced here: 20.2 us
  Pallas kernels  19.4 us (96%)
  local copies, waits for them, and re-layouts  0.73 us (4%)
    pallas_call x1, Pallas kernels, body(): pl.pallas_call(functools.partial(kernel, strips, scenes, strip_cells), ou...  19.4 us
    unnamed x1, local copies, waits for them, and re-layouts  0.73 us

profile of v5, /device:TPU:1, one launch (start us, length us, event | category | flops | bytes accessed | tf_op | source)
XLA Modules:
  0.0 20.2 jit_solution(2662950858809563851)
XLA Ops:
  0.0 19.4 %shard_map.55 = bf16[320,512]{1,0:T(8,128)(2,1)S(1)} custom-call(bf16[80,256]{1,0:T(8,128)(2,1)} %bitcast.8, f32[112,256]{1,0:T(8,128)} %bitcast.7, s32[1,8]{1,0:T(1,128)} %bitcast.11, s32[8,1024]{1,0:T(8,128)} %bitcast.9, s32[8,1024]{1,0:T(8,128)} %bitcast.10), custom_call_target="tpu_custom_call" | custom-call | tf_op jit(solution)/shard_map/pallas_call | solution.py:284
  19.4 0.7 %copy.7 = bf16[512,320]{0,1:T(8,128)(2,1)} copy(bf16[512,320]{0,1:T(8,128)(2,1)S(1)} %bitcast.6) | data formatting | bytes 655360

commit v6 on v5

--- a/solution.py
+++ b/solution.py
@@ -35,6 +35,16 @@
     me = lax.axis_index("bev")
     scene = lax.axis_index("scene")
 
+    barrier = pltpu.get_barrier_semaphore()
+
+    @pl.loop(1, strips)
+    def _(step):
+        pl.semaphore_signal(barrier, inc=1, device_id={"bev": lax.rem(me + step, strips)}, device_id_type=MESH)
+
+    @pl.loop(1, scenes)
+    def _(step):
+        pl.semaphore_signal(barrier, inc=1, device_id={"scene": lax.rem(scene + step, scenes)}, device_id_type=MESH)
+
     loads = [
         pltpu.make_async_copy(src, dst, load.at[i])
         for i, (src, dst) in enumerate([
@@ -44,16 +54,6 @@
     for copy in loads:
         copy.start()
 
-    barrier = pltpu.get_barrier_semaphore()
-
-    @pl.loop(1, strips)
-    def _(step):
-        pl.semaphore_signal(barrier, inc=1, device_id={"bev": lax.rem(me + step, strips)}, device_id_type=MESH)
-
-    @pl.loop(1, scenes)
-    def _(step):
-        pl.semaphore_signal(barrier, inc=1, device_id={"scene": lax.rem(scene + step, scenes)}, device_id_type=MESH)
-
     pl.semaphore_wait(barrier, strips - 1 + scenes - 1)
 
     pair = me + 1 - 2 * lax.rem(me, 2)
@@ -101,7 +101,9 @@
             send_sem=slot_send.at[item], recv_sem=slot_recv.at[source],
             device_id={"bev": source}, device_id_type=MESH).wait_recv()
 
-    @pl.loop(1, half_strips + 1)
+    own_context(half_strips).start()
+
+    @pl.loop(1, half_strips)
     def _(item):
         own_context(item).start()
 
@@ -151,19 +153,13 @@
         context_arrived(item)
         passed_context(item).start()
 
-    fill_two(0)
-    fill_two(1)
-
-    @pl.loop(1, half_strips - 2)
-    def _(item):
-        pass_on(item)
-        fill_two(item + 1)
-
-    pass_on(half_strips - 2)
+    @pl.loop(0, half_strips - 1)
+    def _(step):
+        fill_two(step)
+
     fill(target(strips - 1), sent, target(strips - 1))
     slot_copy(strips - 1).start()
     fill(me, got, me)
-    pass_on(half_strips - 1)
 
     def line(block):
         return jnp.concatenate([block[r:r + 1, :] for r in range(rows)], axis=1)
@@ -195,25 +191,31 @@
     near = scene // group
     far = lax.rem(near + 1, HALVES)
 
-    def form_two(first):
-        made = [form(origin(item)) for item in (first, first + 1)]
+    def pool(*items):
+        made = [form(origin(item)) for item in items]
         return scatter(far, [cell for cell, _ in made], [values for _, values in made])
 
-    slots_arrived(1)
-    total[...] = form_two(0)
-
-    @pl.loop(1, half_strips // 2)
-    def _(step):
-        slots_arrived(2 * step)
-        slots_arrived(2 * step + 1)
-        total[...] += form_two(2 * step)
-
-    @pl.loop(half_strips // 2, half_strips)
-    def _(step):
-        for item in (2 * step, 2 * step + 1):
-            slots_arrived(item)
+    def arrived(item):
+        slots_arrived(item)
+
+        @pl.when(item >= half_strips)
+        def _():
             context_arrived(item)
-        total[...] += form_two(2 * step)
+
+    total[...] = pool(0)
+
+    @pl.loop(1, half_strips)
+    def _(item):
+        pass_on(item)
+
+    @pl.loop(0, half_strips - 1)
+    def _(step):
+        arrived(2 * step + 1)
+        arrived(2 * step + 2)
+        total[...] += pool(2 * step + 1, 2 * step + 2)
+
+    arrived(strips - 1)
+    total[...] += pool(strips - 1)
 
     def pack(half):
         for q in range(group):

time: 20.3 us -> 20.8 us (1.025)
  Pallas kernels: 19.4 us -> 20 us
    pallas_call x1, Pallas kernels: 19.4 us -> 20 us  [body(): pl.pallas_call(functools.partial(kernel, strips, scenes, strip_cells), ou...]
where the time goes in v6:
time: 20.8 us; the launch traced here: 20.7 us
  Pallas kernels  20 us (96%)
  local copies, waits for them, and re-layouts  0.73 us (4%)
    pallas_call x1, Pallas kernels, body(): pl.pallas_call(functools.partial(kernel, strips, scenes, strip_cells), ou...  20 us
    unnamed x1, local copies, waits for them, and re-layouts  0.73 us

profile of v6, /device:TPU:1, one launch (start us, length us, event | category | flops | bytes accessed | tf_op | source)
XLA Modules:
  0.0 20.7 jit_solution(10535688681647834549)
XLA Ops:
  0.0 20.0 %shard_map.55 = bf16[320,512]{1,0:T(8,128)(2,1)S(1)} custom-call(bf16[80,256]{1,0:T(8,128)(2,1)} %bitcast.8, f32[112,256]{1,0:T(8,128)} %bitcast.7, s32[1,8]{1,0:T(1,128)} %bitcast.11, s32[8,1024]{1,0:T(8,128)} %bitcast.9, s32[8,1024]{1,0:T(8,128)} %bitcast.10), custom_call_target="tpu_custom_call" | custom-call | tf_op jit(solution)/shard_map/pallas_call | solution.py:286
  20.0 0.7 %copy.7 = bf16[512,320]{0,1:T(8,128)(2,1)} copy(bf16[512,320]{0,1:T(8,128)(2,1)S(1)} %bitcast.6) | data formatting | bytes 655360

commit v7 on v6

--- a/solution.py
+++ b/solution.py
@@ -60,12 +60,16 @@
     half_strips = strips // 2
 
     def target(item):
-        start = jnp.where(item < half_strips, me, pair)
-        return lax.rem(start + 2 * lax.rem(item, half_strips), strips)
-
-    def origin(item):
-        start = jnp.where(item < half_strips, me, pair)
-        return lax.rem(start + strips - 2 * lax.rem(item, half_strips), strips)
+        item = jnp.int32(item)
+        key = 2 * lax.rem(item, half_strips) + lax.div(item, half_strips)
+        place = jnp.int32(0)
+        for bit in range(log2(strips)):
+            mine = lax.rem(lax.div(me, 2 ** bit), 2)
+            other = lax.rem(lax.div(key, 2 ** bit), 2)
+            place = place + (mine + other - 2 * mine * other) * 2 ** bit
+        return place
+
+    origin = target
 
     def own_context(item):
         return pltpu.make_async_remote_copy(
@@ -153,9 +157,10 @@
         context_arrived(item)
         passed_context(item).start()
 
-    @pl.loop(0, half_strips - 1)
-    def _(step):
-        fill_two(step)
+    @pl.loop(1, half_strips)
+    def _(item):
+        fill_two(item - 1)
+        pass_on(item)
 
     fill(target(strips - 1), sent, target(strips - 1))
     slot_copy(strips - 1).start()
@@ -203,10 +208,6 @@
             context_arrived(item)
 
     total[...] = pool(0)
-
-    @pl.loop(1, half_strips)
-    def _(item):
-        pass_on(item)
 
     @pl.loop(0, half_strips - 1)
     def _(step):

time: 20.8 us -> 21.4 us (1.029)
  Pallas kernels: 20 us -> 20.5 us
    pallas_call x1, Pallas kernels: 20 us -> 20.5 us  [body(): pl.pallas_call(functools.partial(kernel, strips, scenes, strip_cells), ou...]
where the time goes in v7:
time: 21.4 us; the launch traced here: 21.3 us
  Pallas kernels  20.5 us (96%)
  local copies, waits for them, and re-layouts  0.73 us (3%)
    pallas_call x1, Pallas kernels, body(): pl.pallas_call(functools.partial(kernel, strips, scenes, strip_cells), ou...  20.5 us
    unnamed x1, local copies, waits for them, and re-layouts  0.73 us

profile of v7, /device:TPU:1, one launch (start us, length us, event | category | flops | bytes accessed | tf_op | source)
XLA Modules:
  0.0 21.3 jit_solution(11973763262841658663)
XLA Ops:
  0.0 20.5 %shard_map.55 = bf16[320,512]{1,0:T(8,128)(2,1)S(1)} custom-call(bf16[80,256]{1,0:T(8,128)(2,1)} %bitcast.8, f32[112,256]{1,0:T(8,128)} %bitcast.7, s32[1,8]{1,0:T(1,128)} %bitcast.11, s32[8,1024]{1,0:T(8,128)} %bitcast.9, s32[8,1024]{1,0:T(8,128)} %bitcast.10), custom_call_target="tpu_custom_call" | custom-call | tf_op jit(solution)/shard_map/pallas_call | solution.py:287
  20.5 0.7 %copy.7 = bf16[512,320]{0,1:T(8,128)(2,1)} copy(bf16[512,320]{0,1:T(8,128)(2,1)S(1)} %bitcast.6) | data formatting | bytes 655360

commit v8 on v5

--- a/solution.py
+++ b/solution.py
@@ -11,6 +11,7 @@
 LANES = 128
 LOW = 4
 HALVES = 2
+BLOCK = 4
 MESH = pl.DeviceIdType.MESH
 
 
@@ -141,29 +142,32 @@
             slots[place, r:r + 1, :] = weight[:, r * LANES:(r + 1) * LANES]
             slots[place, rows + r:rows + r + 1, :] = code[:, r * LANES:(r + 1) * LANES]
 
-    def fill_two(group):
-        for item in (2 * group + 1, 2 * group + 2):
+    blocks = strips // BLOCK
+    assert strips % (2 * BLOCK) == 0
+
+    def fill_block(block, last):
+        items = [block * BLOCK + i + 1 for i in range(BLOCK - last)]
+        for item in items:
             fill(target(item), sent, target(item))
-        for item in (2 * group + 1, 2 * group + 2):
+        if last:
+            fill(me, got, me)
+        for item in items:
             slot_copy(item).start()
 
     def pass_on(item):
         context_arrived(item)
         passed_context(item).start()
 
-    fill_two(0)
-    fill_two(1)
-
-    @pl.loop(1, half_strips - 2)
+    @pl.loop(0, blocks - 1)
+    def _(block):
+        fill_block(block, 0)
+        pass_on(block + 1)
+
+    fill_block(blocks - 1, 1)
+
+    @pl.loop(blocks, half_strips)
     def _(item):
         pass_on(item)
-        fill_two(item + 1)
-
-    pass_on(half_strips - 2)
-    fill(target(strips - 1), sent, target(strips - 1))
-    slot_copy(strips - 1).start()
-    fill(me, got, me)
-    pass_on(half_strips - 1)
 
     def line(block):
         return jnp.concatenate([block[r:r + 1, :] for r in range(rows)], axis=1)
@@ -195,25 +199,26 @@
     near = scene // group
     far = lax.rem(near + 1, HALVES)
 
-    def form_two(first):
-        made = [form(origin(item)) for item in (first, first + 1)]
+    def pool(block):
+        made = [form(origin(block * BLOCK + i)) for i in range(BLOCK)]
         return scatter(far, [cell for cell, _ in made], [values for _, values in made])
 
-    slots_arrived(1)
-    total[...] = form_two(0)
-
-    @pl.loop(1, half_strips // 2)
-    def _(step):
-        slots_arrived(2 * step)
-        slots_arrived(2 * step + 1)
-        total[...] += form_two(2 * step)
-
-    @pl.loop(half_strips // 2, half_strips)
-    def _(step):
-        for item in (2 * step, 2 * step + 1):
-            slots_arrived(item)
-            context_arrived(item)
-        total[...] += form_two(2 * step)
+    for item in range(1, BLOCK):
+        slots_arrived(item)
+    total[...] = pool(0)
+
+    @pl.loop(1, blocks // 2)
+    def _(block):
+        for i in range(BLOCK):
+            slots_arrived(block * BLOCK + i)
+        total[...] += pool(block)
+
+    @pl.loop(blocks // 2, blocks)
+    def _(block):
+        for i in range(BLOCK):
+            slots_arrived(block * BLOCK + i)
+            context_arrived(block * BLOCK + i)
+        total[...] += pool(block)
 
     def pack(half):
         for q in range(group):
@@ -234,15 +239,15 @@
     for q in range(group):
         part_copy(far * group + q).start()
 
-    def again(first):
-        sources = [2 * first, 2 * first + 1]
+    def again(block):
+        sources = [2 * BLOCK * block + i for i in range(2 * BLOCK)]
         return scatter(near, [decode(source)[1] for source in sources], [values_all[source] for source in sources])
 
     total[...] = again(0)
 
-    @pl.loop(1, half_strips)
-    def _(step):
-        total[...] += again(step)
+    @pl.loop(1, blocks // 2)
+    def _(block):
+        total[...] += again(block)
 
     pack(near)
     others = [near * group + lax.rem(scene + o, group) for o in range(1, group)]

time: 20.3 us -> 21 us (1.034)
  Pallas kernels: 19.4 us -> 20.2 us
    pallas_call x1, Pallas kernels: 19.4 us -> 20.2 us  [body(): pl.pallas_call(functools.partial(kernel, strips, scenes, strip_cells), ou...]
where the time goes in v8:
time: 21 us; the launch traced here: 20.9 us
  Pallas kernels  20.2 us (96%)
  local copies, waits for them, and re-layouts  0.73 us (3%)
    pallas_call x1, Pallas kernels, body(): pl.pallas_call(functools.partial(kernel, strips, scenes, strip_cells), ou...  20.2 us
    unnamed x1, local copies, waits for them, and re-layouts  0.73 us

profile of v8, /device:TPU:1, one launch (start us, length us, event | category | flops | bytes accessed | tf_op | source)
XLA Modules:
  0.0 20.9 jit_solution(3581809747299431221)
XLA Ops:
  0.0 20.2 %shard_map.55 = bf16[320,512]{1,0:T(8,128)(2,1)S(1)} custom-call(bf16[80,256]{1,0:T(8,128)(2,1)} %bitcast.8, f32[112,256]{1,0:T(8,128)} %bitcast.7, s32[1,8]{1,0:T(1,128)} %bitcast.11, s32[8,1024]{1,0:T(8,128)} %bitcast.9, s32[8,1024]{1,0:T(8,128)} %bitcast.10), custom_call_target="tpu_custom_call" | custom-call | tf_op jit(solution)/shard_map/pallas_call | solution.py:289
  20.2 0.7 %copy.7 = bf16[512,320]{0,1:T(8,128)(2,1)} copy(bf16[512,320]{0,1:T(8,128)(2,1)S(1)} %bitcast.6) | data formatting | bytes 655360

commit v9 on v5

--- a/solution.py
+++ b/solution.py
@@ -35,6 +35,16 @@
     me = lax.axis_index("bev")
     scene = lax.axis_index("scene")
 
+    barrier = pltpu.get_barrier_semaphore()
+
+    @pl.loop(1, strips)
+    def _(step):
+        pl.semaphore_signal(barrier, inc=1, device_id={"bev": lax.rem(me + step, strips)}, device_id_type=MESH)
+
+    @pl.loop(1, scenes)
+    def _(step):
+        pl.semaphore_signal(barrier, inc=1, device_id={"scene": lax.rem(scene + step, scenes)}, device_id_type=MESH)
+
     loads = [
         pltpu.make_async_copy(src, dst, load.at[i])
         for i, (src, dst) in enumerate([
@@ -43,16 +53,6 @@
     ]
     for copy in loads:
         copy.start()
-
-    barrier = pltpu.get_barrier_semaphore()
-
-    @pl.loop(1, strips)
-    def _(step):
-        pl.semaphore_signal(barrier, inc=1, device_id={"bev": lax.rem(me + step, strips)}, device_id_type=MESH)
-
-    @pl.loop(1, scenes)
-    def _(step):
-        pl.semaphore_signal(barrier, inc=1, device_id={"scene": lax.rem(scene + step, scenes)}, device_id_type=MESH)
 
     pl.semaphore_wait(barrier, strips - 1 + scenes - 1)
 
@@ -195,25 +195,30 @@
     near = scene // group
     far = lax.rem(near + 1, HALVES)
 
-    def form_two(first):
-        made = [form(origin(item)) for item in (first, first + 1)]
+    def pool(*items):
+        made = [form(origin(item)) for item in items]
         return scatter(far, [cell for cell, _ in made], [values for _, values in made])
 
     slots_arrived(1)
-    total[...] = form_two(0)
+    total[...] = pool(0, 1)
 
     @pl.loop(1, half_strips // 2)
     def _(step):
         slots_arrived(2 * step)
         slots_arrived(2 * step + 1)
-        total[...] += form_two(2 * step)
-
-    @pl.loop(half_strips // 2, half_strips)
+        total[...] += pool(2 * step, 2 * step + 1)
+
+    @pl.loop(half_strips // 2, half_strips - 1)
     def _(step):
         for item in (2 * step, 2 * step + 1):
             slots_arrived(item)
             context_arrived(item)
-        total[...] += form_two(2 * step)
+        total[...] += pool(2 * step, 2 * step + 1)
+
+    for item in (strips - 2, strips - 1):
+        slots_arrived(item)
+        context_arrived(item)
+        total[...] += pool(item)
 
     def pack(half):
         for q in range(group):

time: 20.3 us -> 20.7 us (1.020)
  Pallas kernels: 19.4 us -> 19.8 us
    pallas_call x1, Pallas kernels: 19.4 us -> 19.8 us  [body(): pl.pallas_call(functools.partial(kernel, strips, scenes, strip_cells), ou...]
where the time goes in v9:
time: 20.7 us; the launch traced here: 20.5 us
  Pallas kernels  19.8 us (96%)
  local copies, waits for them, and re-layouts  0.73 us (4%)
    pallas_call x1, Pallas kernels, body(): pl.pallas_call(functools.partial(kernel, strips, scenes, strip_cells), ou...  19.8 us
    unnamed x1, local copies, waits for them, and re-layouts  0.73 us

profile of v9, /device:TPU:1, one launch (start us, length us, event | category | flops | bytes accessed | tf_op | source)
XLA Modules:
  0.0 20.5 jit_solution(10069546532344971753)
XLA Ops:
  0.0 19.8 %shard_map.55 = bf16[320,512]{1,0:T(8,128)(2,1)S(1)} custom-call(bf16[80,256]{1,0:T(8,128)(2,1)} %bitcast.8, f32[112,256]{1,0:T(8,128)} %bitcast.7, s32[1,8]{1,0:T(1,128)} %bitcast.11, s32[8,1024]{1,0:T(8,128)} %bitcast.9, s32[8,1024]{1,0:T(8,128)} %bitcast.10), custom_call_target="tpu_custom_call" | custom-call | tf_op jit(solution)/shard_map/pallas_call | solution.py:289
  19.8 0.7 %copy.7 = bf16[512,320]{0,1:T(8,128)(2,1)} copy(bf16[512,320]{0,1:T(8,128)(2,1)S(1)} %bitcast.6) | data formatting | bytes 655360

commit v10 on v5

--- a/solution.py
+++ b/solution.py
@@ -162,8 +162,8 @@
     pass_on(half_strips - 2)
     fill(target(strips - 1), sent, target(strips - 1))
     slot_copy(strips - 1).start()
+    pass_on(half_strips - 1)
     fill(me, got, me)
-    pass_on(half_strips - 1)
 
     def line(block):
         return jnp.concatenate([block[r:r + 1, :] for r in range(rows)], axis=1)

time: 20.3 us -> 20.3 us (level)
  no operation moved by 1% of the time
where the time goes in v10:
time: 20.3 us; the launch traced here: 20.1 us
  Pallas kernels  19.4 us (96%)
  local copies, waits for them, and re-layouts  0.73 us (4%)
    pallas_call x1, Pallas kernels, body(): pl.pallas_call(functools.partial(kernel, strips, scenes, strip_cells), ou...  19.4 us
    unnamed x1, local copies, waits for them, and re-layouts  0.73 us

profile of v10, /device:TPU:1, one launch (start us, length us, event | category | flops | bytes accessed | tf_op | source)
XLA Modules:
  0.0 20.1 jit_solution(8928493163382033737)
XLA Ops:
  0.0 19.4 %shard_map.55 = bf16[320,512]{1,0:T(8,128)(2,1)S(1)} custom-call(bf16[80,256]{1,0:T(8,128)(2,1)} %bitcast.8, f32[112,256]{1,0:T(8,128)} %bitcast.7, s32[1,8]{1,0:T(1,128)} %bitcast.11, s32[8,1024]{1,0:T(8,128)} %bitcast.9, s32[8,1024]{1,0:T(8,128)} %bitcast.10), custom_call_target="tpu_custom_call" | custom-call | tf_op jit(solution)/shard_map/pallas_call | solution.py:284
  19.4 0.7 %copy.7 = bf16[512,320]{0,1:T(8,128)(2,1)} copy(bf16[512,320]{0,1:T(8,128)(2,1)S(1)} %bitcast.6) | data formatting | bytes 655360
